TPU v7x, 256 devices: a whole 4x4x8 slice. The times are simulated.
256 devices in a mesh: head: 8 (over y, core), seq: 32 (over z, x).
Axes of the slice: x: 4, y: 4, z: 8, core: 2. Of those that a mesh axis runs over, the one named last changes fastest.
Arguments:
- queries: bfloat16 [32768, 2048], P('seq', 'head'), may hold values from -4 to 4
- keys: bfloat16 [32768, 2048], P('seq', 'head'), may hold values from -4 to 4
- values: bfloat16 [32768, 4096], P('seq', 'head'), may hold values from -6 to 6
- input_gate: float32 [32768, 8], P('seq', 'head'), may hold values from -4 to 4
- forget_gate: float32 [32768, 8], P('seq', 'head')
- out_weight: bfloat16 [4096, 4096], P('head', 'seq'), may hold values from -0.09375 to 0.09375
Outputs:
- mixed: bfloat16 [32768, 4096], P('seq', 'head')
All inputs are finite; a program needn't handle non-finite values.
Results may differ from a plain program's by a relative error of at most 0.019.
Values may be sent and summed in bfloat16 or wider, within the bound.
A program may use at most 128 MiB of HBM per device.

v0:
```python
import jax
import jax.numpy as jnp
from jax import lax
from jax.sharding import PartitionSpec as P

WINDOW = 1024
PRECISE = lax.Precision.HIGHEST
VERY_NEGATIVE = -1e30


def from_behind(block, axis, distance):
    devices = range(lax.axis_size(axis))
    route = [(i - distance, i) for i in devices if i - distance in devices]
    return lax.ppermute(block, axis, route)


def entering(part, axis, combine, identity):
    place = lax.axis_index(axis)
    gathered = jax.tree.map(lambda a: lax.all_gather(a, axis), part)
    state = jax.tree.map(lambda a, e: jnp.zeros_like(a) + jnp.asarray(e, a.dtype), part, identity)

    def one(hop, state):
        return combine(
            state, jax.tree.map(lambda a: lax.dynamic_index_in_dim(a, hop, 0, False), gathered)
        )

    return lax.fori_loop(0, place, one, state)


def memory_block(query_rows, key_rows, value_rows, gate_keys, cum_query, cum_key, carry_state):
    mem_c, mem_n, mem_m = carry_state
    key_scale = query_rows.shape[-1] ** (-0.5)
    scores = jnp.dot(query_rows, key_rows.T, preferred_element_type=jnp.float32) * key_scale
    query_index = jnp.arange(query_rows.shape[0], dtype=jnp.int32)
    key_index = jnp.arange(key_rows.shape[0], dtype=jnp.int32)
    causal = key_index[None, :] <= query_index[:, None]
    log_decay = jnp.where(
        causal, cum_query[:, None] - cum_key[None, :] + gate_keys[None, :], VERY_NEGATIVE
    )
    carry_log = cum_query + mem_m
    mem_max = jnp.maximum(jnp.max(log_decay, axis=1), carry_log)
    decays = jnp.where(causal, jnp.exp(log_decay - mem_max[:, None]), 0.0)
    weighted = decays * scores
    carry_scale = jnp.exp(carry_log - mem_max)
    query_full = query_rows.astype(jnp.float32) * key_scale
    numerator = jnp.dot(
        weighted.astype(jnp.bfloat16), value_rows, preferred_element_type=jnp.float32
    )
    numerator = numerator + carry_scale[:, None] * jnp.dot(query_full, mem_c, precision=PRECISE)
    denominator = jnp.sum(weighted, axis=1) + carry_scale * jnp.dot(
        query_full, mem_n, precision=PRECISE
    )
    return (numerator, denominator, mem_max)


def window_block(query_rows, key_window, value_window, query_pos, key_pos, mem_max):
    key_scale = query_rows.shape[-1] ** (-0.5)
    scores = jnp.dot(query_rows, key_window.T, preferred_element_type=jnp.float32) * key_scale
    visible = (
        (key_pos[None, :] <= query_pos[:, None])
        & (key_pos[None, :] > query_pos[:, None] - WINDOW)
        & (key_pos[None, :] >= 0)
    )
    top_score = jnp.max(jnp.where(visible, scores, VERY_NEGATIVE), axis=1)
    joint_max = jnp.maximum(top_score, mem_max)
    weights = jnp.where(visible, jnp.exp(scores - joint_max[:, None]), 0.0)
    numerator = jnp.dot(
        weights.astype(jnp.bfloat16), value_window, preferred_element_type=jnp.float32
    )
    return (numerator, jnp.sum(weights, axis=1), joint_max)


def joint_output(window, memory):
    win_num, win_den, joint_max = window
    mem_num, mem_den, mem_max = memory
    lifted = jnp.exp(mem_max - joint_max)
    bottom = win_den + lifted * jnp.maximum(jnp.abs(mem_den), 1.0)
    return ((win_num + lifted[:, None] * mem_num) / bottom[:, None]).astype(jnp.bfloat16)


def span_summary(key_rows, value_rows, gate_keys, cum_key):
    total_decay = cum_key[-1]
    log_weight = total_decay - cum_key + gate_keys
    new_max = jnp.max(log_weight)
    scaled_keys = key_rows.astype(jnp.float32) * jnp.exp(log_weight - new_max)[:, None]
    mem_c = jnp.dot(scaled_keys.T, value_rows.astype(jnp.float32), precision=PRECISE)
    return (mem_c, jnp.sum(scaled_keys, axis=0), new_max, total_decay)


def merge_states(older, newer):
    lifted = newer[3] + older[2]
    new_max = jnp.maximum(lifted, newer[2])
    old_weight = jnp.exp(lifted - new_max)
    new_weight = jnp.exp(newer[2] - new_max)
    mem_c = old_weight[..., None, None] * older[0] + new_weight[..., None, None] * newer[0]
    mem_n = old_weight[..., None] * older[1] + new_weight[..., None] * newer[1]
    return (mem_c, mem_n, new_max, older[3] + newer[3])


def split_heads(matrix, head_count):
    return matrix.reshape(matrix.shape[0], head_count, matrix.shape[1] // head_count).transpose(
        1, 0, 2
    )


def local(queries, keys, values, input_gate, forget_gate, out_weight):
    row_count = queries.shape[0]
    local_heads = input_gate.shape[1]
    tail_pair = (keys, values)
    pieces = [from_behind((tail_pair[0], tail_pair[1]), "seq", 1)]
    ext_keys = jnp.concatenate([entry[0] for entry in pieces[::-1]] + [keys], axis=0)
    ext_values = jnp.concatenate([entry[1] for entry in pieces[::-1]] + [values], axis=0)
    query_heads = split_heads(queries, local_heads)
    key_heads = split_heads(keys, local_heads)
    value_heads = split_heads(values, local_heads)
    ext_key_heads = split_heads(ext_keys, local_heads)
    ext_value_heads = split_heads(ext_values, local_heads)
    gate_heads = input_gate.T
    cum_heads = jnp.cumsum(jax.nn.log_sigmoid(forget_gate.T), axis=1)
    summaries = jax.vmap(span_summary)(key_heads, value_heads, gate_heads, cum_heads)
    identity = (
        jnp.zeros_like(summaries[0]),
        jnp.zeros_like(summaries[1]),
        jnp.full_like(summaries[2], VERY_NEGATIVE),
        jnp.zeros_like(summaries[3]),
    )
    carried = entering(summaries, "seq", merge_states, identity)
    base_pos = lax.axis_index("seq") * row_count
    block_rows = min(row_count, 512)

    def head_output(
        query_all, key_all, value_all, key_ext, value_ext, gate_keys, cum_gate, mem_c, mem_n, mem_m
    ):
        results = []
        state = (mem_c, mem_n, mem_m, jnp.zeros_like(mem_m))
        for block_index in range(row_count // block_rows):
            first_row = block_index * block_rows
            last_row = first_row + block_rows
            query_rows = query_all[first_row:last_row]
            key_rows = key_all[first_row:last_row]
            value_rows = value_all[first_row:last_row]
            gate_rows = gate_keys[first_row:last_row]
            local_cum = cum_gate[first_row:last_row]
            if first_row > 0:
                local_cum = local_cum - cum_gate[first_row - 1]
            memory = memory_block(
                query_rows, key_rows, value_rows, gate_rows, local_cum, local_cum, state[:3]
            )
            key_window = key_ext[first_row : last_row + WINDOW]
            value_window = value_ext[first_row : last_row + WINDOW]
            query_pos = base_pos + first_row + jnp.arange(block_rows, dtype=jnp.int32)
            key_pos = (
                base_pos + first_row - WINDOW + jnp.arange(WINDOW + block_rows, dtype=jnp.int32)
            )
            window = window_block(
                query_rows, key_window, value_window, query_pos, key_pos, memory[2]
            )
            results.append(joint_output(window, memory))
            if last_row < row_count:
                state = merge_states(
                    state, span_summary(key_rows, value_rows, gate_rows, local_cum)
                )
        return jnp.concatenate(results, axis=0)

    hidden_heads = jax.vmap(head_output)(
        query_heads,
        key_heads,
        value_heads,
        ext_key_heads,
        ext_value_heads,
        gate_heads,
        cum_heads,
        carried[0],
        carried[1],
        carried[2],
    )
    hidden = hidden_heads.transpose(1, 0, 2).reshape(row_count, local_heads * hidden_heads.shape[2])
    partial_terms = jnp.dot(
        hidden,
        lax.all_gather(out_weight, "seq", axis=1, tiled=True),
        preferred_element_type=jnp.float32,
    )
    mixed = lax.psum_scatter(
        partial_terms.astype(jnp.bfloat16), "head", scatter_dimension=1, tiled=True
    )
    return mixed


def solution(mesh):
    placed = (
        P("seq", "head"),
        P("seq", "head"),
        P("seq", "head"),
        P("seq", "head"),
        P("seq", "head"),
        P("head", "seq"),
    )
    return jax.shard_map(
        local, mesh=mesh, in_specs=placed, out_specs=P("seq", "head"), check_vma=False
    )
```

profile of v0, /device:TPU:1, one launch (start us, length us, event | category | flops | bytes accessed | tf_op | source)
XLA Modules:
  0.0 400.4 jit_solution(119145561673392502)
XLA Ops:
  8.7 1.9 add_reduce_fusion
  10.7 2.0 fusion.89
  12.6 3.5 fusion.42
  16.3 4.0 collective-permute-start
  20.2 3.2 collective-permute-start.1
  24.2 1.2 dynamic-slice
  25.5 1.2 bitcast_dynamic-update-slice_fusion
  26.7 1.3 dynamic-update-slice.1
  28.0 97.5 %all-reduce.2 = (f32[32]{0:T(128)S(1)}, f32[32]{0:T(128)S(1)}) all-reduce(f32[32]{0:T(128)S(1)} %bitcast_dynamic-update-slice_fusion, f32[32]{0:T(128)S(1)} %dynamic-update-slice.1), channel_id=1, replica_groups=mesh['head'=8,'seq'=32] {'seq'}, use_global_device_ids=true, to_apply=%add | all-reduce | flops 64 | bytes 512
  126.0 41.6 %all-gather.2 = f32[32,1,256]{2,1,0:T(1,128)S(1)} all-gather(f32[1,1,256]{2,1,0:T(1,128)S(1)} %bitcast.249), channel_id=3, replica_groups=mesh['head'=8,'seq'=32] {'seq'}, dimensions={0}, use_global_device_ids=true | all-gather | bytes 33792 | tf_op jit(solution)/shard_map/all_gather | solution.py:19
  167.7 3.0 select_reduce_fusion.1
  170.8 3.0 select_reduce_fusion
  173.8 1.4 maximum_bitcast_fusion
  176.4 0.8 subtract_exponential_fusion.4
  177.2 1.3 fusion.102
  182.2 1.5 fusion.2
  184.7 1.5 fusion.4
  187.8 1.1 fusion.17
  188.9 1.1 fusion.15
  190.0 1.9 fusion.50
  191.9 1.8 fusion.45
  193.7 60.6 %all-gather.6.cloned.1.call-done = bf16[512,4096]{1,0:T(8,128)(2,1)} async-done(((bf16[512,128]{1,0:T(8,128)(2,1)}), bf16[512,4096]{1,0:T(8,128)(2,1)}) %all-gather.6.cloned.1.call-update) | async-done | bytes 4194320 | tf_op jit(solution)/shard_map/all_gather | solution.py:180
  254.3 9.6 %convolution_convert_fusion = bf16[1024,4096]{1,0:T(8,128)(2,1)} fusion(bf16[512,4096]{1,0:T(8,128)(2,1)} %all-gather.6.cloned.1.call-done, bf16[1,512,512]{2,1,0:T(8,128)(2,1)S(1)} %fusion.45, bf16[1,512,512]{2,1,0:T(8,128)(2,1)S(1)} %fusion.50), kind=kOutput, calls=%fused_computation.4 | convolution fusion | flops 4301258752 | bytes 13631488 | tf_op jit(solution)/shard_map/dot_general | solution.py:178
  263.9 129.9 %reduce-scatter.2.cloned.1.call-done = bf16[1024,512]{1,0:T(8,128)(2,1)} async-done(((bf16[1024,4096]{1,0:T(8,128)(2,1)}), bf16[1024,512]{1,0:T(8,128)(2,1)}) %reduce-scatter.2.cloned.1.call-update) | async-done | bytes 1048592 | tf_op jit(solution)/shard_map/reduce_scatter | solution.py:183
  (65 shorter events, 8.7 us)
Async XLA Ops:
  6.5 119.0 %copy-start.1 = (bf16[1024,256]{1,0:T(8,128)(2,1)S(1)}, bf16[1024,256]{1,0:T(8,128)(2,1)}, u32[]{:S(2)}) copy-start(bf16[1024,256]{1,0:T(8,128)(2,1)} %param.9) | copy-start | bytes 1572868
  6.5 161.2 %copy-start.5 = (bf16[1024,256]{1,0:T(8,128)(2,1)S(1)}, bf16[1024,256]{1,0:T(8,128)(2,1)}, u32[]{:S(2)}) copy-start(bf16[1024,256]{1,0:T(8,128)(2,1)} %param.8) | copy-start | bytes 1572868
  6.5 168.7 %all-gather.8.cloned.1.call-start = ((), (), s32[]{:S(2)}) async-start(), calls=%async_computation.3 | async-start | bytes 17301504 | tf_op jit(solution)/shard_map/all_gather | solution.py:19
  16.2 238.1 %all-gather.6.cloned.1.call-start = ((), (), s32[]{:S(2)}) async-start(), calls=%async_computation.1 | async-start | bytes 4325376 | tf_op jit(solution)/shard_map/all_gather | solution.py:180
  16.3 151.4 %collective-permute-start = (bf16[1024,256]{1,0:T(8,128)(2,1)}, bf16[1024,256]{1,0:T(8,128)(2,1)S(1)}, u32[]{:S(2)}, u32[]{:S(2)}) collective-permute-start(bf16[1024,256]{1,0:T(8,128)(2,1)} %param.9), channel_id=1, source_target_pairs={{0,1},{1,2},{2,3},{3,4},{4,5},{5,6},{6,7},{7,8},{8,9},{9,10},{10,1... | collective-permute-start | bytes 1572872 | tf_op jit(solution)/shard_map/ppermute | solution.py:14
  20.2 153.6 %collective-permute-start.1 = (bf16[1024,512]{1,0:T(8,128)(2,1)}, bf16[1024,512]{1,0:T(8,128)(2,1)S(1)}, u32[]{:S(2)}, u32[]{:S(2)}) collective-permute-start(bf16[1024,512]{1,0:T(8,128)(2,1)} %param.10), channel_id=1, source_target_pairs={{0,1},{1,2},{2,3},{3,4},{4,5},{5,6},{6,7},{7,8},{8,9},{9,10},{10,1... | collective-permute-start | bytes 3145736 | tf_op jit(solution)/shard_map/ppermute | solution.py:14
  23.4 370.4 %reduce-scatter.2.cloned.1.call-start = ((), (), s32[]{:S(2)}) async-start(), calls=%async_computation.2 | async-start | bytes 9437184 | tf_op jit(solution)/shard_map/reduce_scatter | solution.py:183
  167.7 3.0 copy-start.6
  170.8 3.0 copy-start
  175.3 1.9 copy-start.8
  175.3 6.4 %copy-start.7 = (bf16[1024,256]{1,0:T(8,128)(2,1)S(1)}, bf16[1024,256]{1,0:T(8,128)(2,1)}, u32[]{:S(2)}) copy-start(bf16[1024,256]{1,0:T(8,128)(2,1)} %param.8) | copy-start | bytes 1572868
  175.5 6.6 %copy-start.3 = (f32[512,1536]{0,1:T(8,128)S(1)}, f32[512,1536]{0,1:T(8,128)}, u32[]{:S(2)}) copy-start(f32[512,1536]{0,1:T(8,128)} %get-tuple-element.156) | copy-start | bytes 9437188
  182.2 2.5 copy-start.2
  187.8 2.3 copy-start.4
Sparse Core Ops, SparseCore 0:
  16.3 158.3 all-gather.7
  177.2 77.0 all-gather.5
  264.0 129.7 reduce-scatter.1
where the time goes:
time: 403 us; the launch traced here: 400 us
  waiting for transfers between devices  191 us (47%)
  blocking collectives  139 us (34%)
  matrix products  28.8 us (7%)
  between operations  15.6 us (4%)
  other arithmetic  13.3 us (3%)
  starting transfers between devices  7.22 us (2%)
  local copies, waits for them, and re-layouts  5.45 us (1%)
    reduce_scatter x1, waiting for transfers between devices, local(): lax.psum_scatter(partial_terms.astype(jnp.bfloat16), 'head', scatter_dime...  130 us
    unnamed x1, blocking collectives  97.5 us
    all_gather x1, waiting for transfers between devices, local(): lax.all_gather(out_weight, 'seq', axis=1, tiled=True)  60.6 us
    all_gather x1, blocking collectives, entering(): gathered = jax.tree.map(lambda a: lax.all_gather(a, axis), part)  41.6 us
    dot_general x1, matrix products, local(): jnp.dot(hidden, lax.all_gather(out_weight, 'seq', axis=1, tiled=True), pr...  9.6 us
  transfers between devices with their start and end apart: 5, of which 2 were waited for; matrix products, arithmetic and copies ran while one was open for 7% of the time, Pallas kernels for 0%

commit v1 on v0

--- a/solution.py
+++ b/solution.py
@@ -177,7 +177,9 @@
     hidden = hidden_heads.transpose(1, 0, 2).reshape(row_count, local_heads * hidden_heads.shape[2])
     partial_terms = jnp.dot(
         hidden,
-        lax.all_gather(out_weight, "seq", axis=1, tiled=True),
+        jnp.concatenate(
+            lax.all_to_all(jnp.stack([out_weight] * lax.axis_size("seq")), "seq", 0, 0), axis=1
+        ),
         preferred_element_type=jnp.float32,
     )
     mixed = lax.psum_scatter(

time: 403 us -> 515 us (1.28)
  blocking collectives: 139 us -> 234 us
  starting transfers between devices: 7.22 us -> 17.6 us
    unnamed x1, blocking collectives: 97.5 us -> 202 us
    reduce_scatter x1, waiting for transfers between devices: 130 us -> 195 us  [local(): lax.psum_scatter(partial_terms.astype(jnp.bfloat16), 'head', scatter_dime...]
    all_gather x1 -> x0, waiting for transfers between devices: 60.6 us -> none  [local(): lax.all_gather(out_weight, 'seq', axis=1, tiled=True)]
    all_to_all x0 -> x1, starting transfers between devices: none -> 10.4 us  [local(): lax.all_to_all(jnp.stack([out_weight] * lax.axis_size('seq')), 'seq', 0, 0)]
    all_gather x1, blocking collectives: 41.6 us -> 32.1 us  [entering(): gathered = jax.tree.map(lambda a: lax.all_gather(a, axis), part)]
  transfers between devices with their start and end apart: 5 -> 5, of which waited for: 2 -> 1; matrix products, arithmetic and copies ran while one was open for 7% -> 6% of each run, Pallas kernels for 0% -> 0%
where the time goes in v1:
time: 515 us; the launch traced here: 513 us
  blocking collectives  234 us (45%)
  waiting for transfers between devices  195 us (38%)
  matrix products  28.8 us (6%)
  starting transfers between devices  17.6 us (3%)
  between operations  16 us (3%)
  other arithmetic  13.2 us (3%)
  local copies, waits for them, and re-layouts  7.67 us (1%)
    unnamed x1, blocking collectives  202 us
    reduce_scatter x1, waiting for transfers between devices, local(): lax.psum_scatter(partial_terms.astype(jnp.bfloat16), 'head', scatter_dime...  195 us
    all_gather x1, blocking collectives, entering(): gathered = jax.tree.map(lambda a: lax.all_gather(a, axis), part)  32.1 us
    all_to_all x1, starting transfers between devices, local(): lax.all_to_all(jnp.stack([out_weight] * lax.axis_size('seq')), 'seq', 0, 0)  10.4 us
  transfers between devices with their start and end apart: 5, of which 1 were waited for; matrix products, arithmetic and copies ran while one was open for 6% of the time, Pallas kernels for 0%

profile of v1, /device:TPU:1, one launch (start us, length us, event | category | flops | bytes accessed | tf_op | source)
XLA Modules:
  0.0 512.5 jit_solution(3924135511577097506)
XLA Ops:
  8.6 1.9 add_reduce_fusion
  10.6 1.9 fusion.89
  12.5 3.5 fusion.42
  16.1 4.0 collective-permute-start
  20.1 3.2 collective-permute-start.1
  23.2 1.0 copy.13
  24.2 2.4 stack.2
  26.7 10.4 %all-to-all-start = ((bf16[32,512,128]{1,2,0:T(8,128)(2,1)}), bf16[32,512,128]{1,2,0:T(8,128)(2,1)}, u32[]{:S(2)}, u32[]{:S(2)}) async-start(bf16[32,512,128]{1,2,0:T(8,128)(2,1)} %stack.2), calls=%async_computation | async-start | bytes 8388608 | tf_op jit(solution)/shard_map/all_to_all | solution.py:181
  37.9 1.3 bitcast_dynamic-update-slice_fusion
  39.2 1.3 dynamic-update-slice.1
  40.5 202.1 %all-reduce.2 = (f32[32]{0:T(128)S(1)}, f32[32]{0:T(128)S(1)}) all-reduce(f32[32]{0:T(128)S(1)} %bitcast_dynamic-update-slice_fusion, f32[32]{0:T(128)S(1)} %dynamic-update-slice.1), channel_id=1, replica_groups=mesh['head'=8,'seq'=32] {'seq'}, use_global_device_ids=true, to_apply=%add | all-reduce | flops 64 | bytes 512
  243.0 32.1 %all-gather.2 = f32[32,1,256]{2,1,0:T(1,128)S(1)} all-gather(f32[1,1,256]{2,1,0:T(1,128)S(1)} %bitcast.252), channel_id=3, replica_groups=mesh['head'=8,'seq'=32] {'seq'}, dimensions={0}, use_global_device_ids=true | all-gather | bytes 33792 | tf_op jit(solution)/shard_map/all_gather | solution.py:19
  275.2 3.0 select_reduce_fusion.1
  278.2 3.1 select_reduce_fusion
  281.3 1.5 maximum_bitcast_fusion
  284.7 1.3 fusion.102
  289.7 1.5 fusion.2
  292.2 1.5 fusion.4
  295.3 1.1 fusion.17
  296.4 1.1 fusion.15
  297.5 1.8 fusion.50
  299.3 1.8 fusion.45
  301.1 9.6 %convolution_convert_fusion = bf16[1024,4096]{1,0:T(8,128)(2,1)} fusion(bf16[512,4096]{0,1:T(8,128)(2,1)} %bitcast.87, bf16[1,512,512]{2,1,0:T(8,128)(2,1)S(1)} %fusion.45, bf16[1,512,512]{2,1,0:T(8,128)(2,1)S(1)} %fusion.50), kind=kOutput, calls=%fused_computation.4 | convolution fusion | flops 4301258752 | bytes 13631488 | tf_op jit(solution)/shard_map/dot_general | solution.py:178
  310.8 194.9 %reduce-scatter.2.cloned.1.call-done = bf16[1024,512]{1,0:T(8,128)(2,1)} async-done(((bf16[1024,4096]{1,0:T(8,128)(2,1)}), bf16[1024,512]{1,0:T(8,128)(2,1)}) %reduce-scatter.2.cloned.1.call-update) | async-done | bytes 1048592 | tf_op jit(solution)/shard_map/reduce_scatter | solution.py:185
  (68 shorter events, 9.2 us)
Async XLA Ops:
  6.5 276.3 %all-gather.5.cloned.1.call-start = ((), (), s32[]{:S(2)}) async-start(), calls=%async_computation.3 | async-start | bytes 17301504 | tf_op jit(solution)/shard_map/all_gather | solution.py:19
  16.1 259.0 %collective-permute-start = (bf16[1024,256]{1,0:T(8,128)(2,1)}, bf16[1024,256]{1,0:T(8,128)(2,1)S(1)}, u32[]{:S(2)}, u32[]{:S(2)}) collective-permute-start(bf16[1024,256]{1,0:T(8,128)(2,1)} %param.9), channel_id=1, source_target_pairs={{0,1},{1,2},{2,3},{3,4},{4,5},{5,6},{6,7},{7,8},{8,9},{9,10},{10,1... | collective-permute-start | bytes 1572872 | tf_op jit(solution)/shard_map/ppermute | solution.py:14
  20.1 261.3 %collective-permute-start.1 = (bf16[1024,512]{1,0:T(8,128)(2,1)}, bf16[1024,512]{1,0:T(8,128)(2,1)S(1)}, u32[]{:S(2)}, u32[]{:S(2)}) collective-permute-start(bf16[1024,512]{1,0:T(8,128)(2,1)} %param.10), channel_id=1, source_target_pairs={{0,1},{1,2},{2,3},{3,4},{4,5},{5,6},{6,7},{7,8},{8,9},{9,10},{10,1... | collective-permute-start | bytes 3145736 | tf_op jit(solution)/shard_map/ppermute | solution.py:14
  26.7 10.5 %copy-start.8 = (f32[1024,1]{0,1:T(1,128)S(1)}, f32[1024,1]{0,1:T(1,128)}, u32[]{:S(2)}) copy-start(f32[1024,1]{0,1:T(1,128)} %param.11) | copy-start | bytes 12292
  26.7 10.5 %copy-start.9 = (u32[256]{0:T(256)S(1)}, u32[256]{0:T(256)}, u32[]{:S(2)}) copy-start(u32[256]{0:T(256)} %constant.67) | copy-start | bytes 3076
  26.7 215.9 %copy-start.1 = (bf16[1024,256]{1,0:T(8,128)(2,1)S(1)}, bf16[1024,256]{1,0:T(8,128)(2,1)}, u32[]{:S(2)}) copy-start(bf16[1024,256]{1,0:T(8,128)(2,1)} %param.9) | copy-start | bytes 1572868
  26.7 248.5 %copy-start.5 = (bf16[1024,256]{1,0:T(8,128)(2,1)S(1)}, bf16[1024,256]{1,0:T(8,128)(2,1)}, u32[]{:S(2)}) copy-start(bf16[1024,256]{1,0:T(8,128)(2,1)} %param.8) | copy-start | bytes 1572868
  26.7 274.4 %all-to-all-start = ((bf16[32,512,128]{1,2,0:T(8,128)(2,1)}), bf16[32,512,128]{1,2,0:T(8,128)(2,1)}, u32[]{:S(2)}, u32[]{:S(2)}) async-start(bf16[32,512,128]{1,2,0:T(8,128)(2,1)} %stack.2), calls=%async_computation | async-start | bytes 8388608 | tf_op jit(solution)/shard_map/all_to_all | solution.py:181
  37.1 468.5 %reduce-scatter.2.cloned.1.call-start = ((), (), s32[]{:S(2)}) async-start(), calls=%async_computation.2 | async-start | bytes 9437184 | tf_op jit(solution)/shard_map/reduce_scatter | solution.py:185
  275.2 3.0 copy-start.6
  278.2 3.1 copy-start
  282.9 6.4 %copy-start.7 = (bf16[1024,256]{1,0:T(8,128)(2,1)S(1)}, bf16[1024,256]{1,0:T(8,128)(2,1)}, u32[]{:S(2)}) copy-start(bf16[1024,256]{1,0:T(8,128)(2,1)} %param.8) | copy-start | bytes 1572868
  283.1 6.6 %copy-start.3 = (f32[512,1536]{0,1:T(8,128)S(1)}, f32[512,1536]{0,1:T(8,128)}, u32[]{:S(2)}) copy-start(f32[512,1536]{0,1:T(8,128)} %get-tuple-element.156) | copy-start | bytes 9437188
  289.7 2.5 copy-start.2
  295.2 2.2 copy-start.4
Sparse Core Ops, SparseCore 0:
  16.2 219.2 all-gather.4
  310.9 194.7 reduce-scatter.1
